TPU v7x, 128 devices: a whole 4x4x4 slice. The times are simulated.
128 devices in a mesh: row: 8 (over x, core), col: 16 (over y, z).
Axes of the slice: x: 4, y: 4, z: 4, core: 2. Of those that a mesh axis runs over, the one named last changes fastest.
Arguments:
- left_tiles: bfloat16 [8192, 4096], P('row', 'col'), may hold values from -6 to 6
- right_tiles: bfloat16 [4096, 16384], P('row', 'col'), may hold values from -0.09375 to 0.09375
- left_mask: int32 [64, 32], P('row', 'col'), may hold values from 0 to 1, as said below
- right_mask: int32 [32, 128], P('row', 'col'), may hold values from 0 to 1, as said below
- cycle_weight: bfloat16 [16384, 1024], P('col', 'row'), may hold values from -0.046875 to 0.046875
Outputs:
- cycle_out: float32 [64, 128, 1024], P('row', 'col')
Inputs may be any that keep to these rules, and one draw needn't show every extreme that they name: `left_mask`: each tile row i keeps each of its tiles with chance one, two or three thirds, the level drawn per row. `right_mask`: each tile column a keeps each of its tiles with chance one, two or three thirds, the level drawn per column.
All inputs are finite; a program needn't handle non-finite values.
Results may differ from a plain program's by a relative error of at most 0.0029.
Values may be sent and summed in bfloat16 or wider, within the bound.
A program may use at most 64 MiB of HBM per device.

v0:
```python
import jax
import jax.numpy as jnp
from jax import lax
from jax.sharding import PartitionSpec as P

JOCC = 128
VIRT_B = 128


def apply_mask(tiles, mask):
    rows, cols = tiles.shape
    mrows, mcols = mask.shape
    shaped = tiles.reshape(mrows, rows // mrows, mcols, cols // mcols)
    return (shaped * mask[:, None, :, None].astype(tiles.dtype)).reshape(rows, cols)


def body(left_tiles, right_tiles, left_mask, right_mask, cycle_weight):
    masked_left = apply_mask(left_tiles, left_mask)
    masked_right = apply_mask(right_tiles, right_mask)
    gathered = lax.all_gather(masked_left, "col", axis=1, tiled=True)
    totals = jnp.dot(
        gathered,
        lax.all_gather(masked_right, "row", axis=0, tiled=True),
        preferred_element_type=jnp.float32,
    )
    occ_local = left_mask.shape[0]
    vir_local = right_mask.shape[1]
    pair_block = totals.astype(jnp.bfloat16).reshape(occ_local, JOCC, vir_local, VIRT_B)
    relaid = lax.all_to_all(pair_block, "col", split_axis=1, concat_axis=2, tiled=True)
    piece = lax.all_gather(cycle_weight, "row", axis=1, tiled=True)
    operand = piece.reshape(piece.shape[0] // VIRT_B, VIRT_B, piece.shape[1])
    cycle_terms = jnp.einsum("ijab,jbk->iak", relaid, operand, preferred_element_type=jnp.float32)
    return lax.psum_scatter(cycle_terms, "col", scatter_dimension=1, tiled=True)


def solution(mesh):
    placed = (P("row", "col"), P("row", "col"), P("row", "col"), P("row", "col"), P("col", "row"))
    return jax.shard_map(
        body, mesh=mesh, in_specs=placed, out_specs=P("row", "col", None), check_vma=False
    )
```

profile of v0, /device:TPU:0, one launch (start us, length us, event | category | flops | bytes accessed | tf_op | source)
XLA Modules:
  0.0 281.0 jit_solution(11570222039503494329)
XLA Ops:
  6.5 0.0 all-gather.6.cloned.1.call-start
  6.5 0.7 convert_element_type.12
  7.2 0.2 mul.25
  7.4 0.0 copy-start.1
  7.4 0.0 copy-start
  7.5 2.4 bitcast_multiply_fusion
  9.9 0.0 all-gather.6.cloned.1.call-update
  9.9 0.0 all-gather.4.cloned.1.call-start
  9.9 0.0 copy-done.1
  9.9 0.1 copy.8
  10.0 0.3 mul.22
  10.4 0.0 copy-done
  10.4 0.9 bitcast_multiply_fusion.1
  11.3 0.0 all-gather.4.cloned.1.call-update
  11.3 0.0 all-gather.8.cloned.1.call-start
  11.4 0.7 all-gather.8.cloned.1.call-update
  12.0 50.1 %all-gather.6.cloned.1.call-done = bf16[4096,1024]{1,0:T(8,128)(2,1)} async-done(((bf16[512,1024]{1,0:T(8,128)(2,1)}), bf16[4096,1024]{1,0:T(8,128)(2,1)}) %all-gather.6.cloned.1.call-update) | async-done | bytes 8388624 | tf_op jit(solution)/shard_map/all_gather | solution.py:23
  62.2 80.9 %all-gather.4.cloned.1.call-done = bf16[1024,4096]{1,0:T(8,128)(2,1)} async-done(((bf16[1024,256]{1,0:T(8,128)(2,1)}), bf16[1024,4096]{1,0:T(8,128)(2,1)}) %all-gather.4.cloned.1.call-update) | async-done | bytes 8388624 | tf_op jit(solution)/shard_map/all_gather | solution.py:20
  143.0 13.7 %convert_bitcast_fusion = bf16[128,8,8,128]{3,1,2,0:T(8,128)(2,1)S(1)} fusion(bf16[1024,4096]{1,0:T(8,128)(2,1)} %all-gather.4.cloned.1.call-done, bf16[4096,1024]{1,0:T(8,128)(2,1)} %all-gather.6.cloned.1.call-done), kind=kOutput, calls=%fused_computation.3 | convolution fusion | flops 8590983168 | bytes 18874368 | tf_op jit(solution)/shard_map/dot_general | solution.py:21
  156.7 0.6 copy.14
  157.3 1.9 copy.9
  159.3 4.9 %all-to-all-start = ((bf16[8,128,8,128]{3,2,0,1:T(8,128)(2,1)}), bf16[8,128,8,128]{3,2,0,1:T(8,128)(2,1)S(1)}, u32[]{:S(2)}, u32[]{:S(2)}) async-start(bf16[8,128,8,128]{3,2,0,1:T(8,128)(2,1)} %copy.9), calls=%async_computation | async-start | bytes 4194304 | tf_op jit(solution)/shard_map/all_to_all | solution.py:29
  164.2 0.0 reduce-scatter.2.cloned.1.call-start
  164.3 6.9 %all-gather.8.cloned.1.call-done = bf16[1024,1024]{1,0:T(8,128)(2,1)} async-done(((bf16[1024,128]{1,0:T(8,128)(2,1)}), bf16[1024,1024]{1,0:T(8,128)(2,1)}) %all-gather.8.cloned.1.call-update) | async-done | bytes 2097168 | tf_op jit(solution)/shard_map/all_gather | solution.py:30
  171.2 21.9 %all-to-all-done = bf16[8,128,8,128]{3,2,0,1:T(8,128)(2,1)S(1)} async-done(((bf16[8,128,8,128]{3,2,0,1:T(8,128)(2,1)}), bf16[8,128,8,128]{3,2,0,1:T(8,128)(2,1)S(1)}, u32[]{:S(2)}, u32[]{:S(2)}) %all-to-all-start) | async-done | bytes 2097184 | tf_op jit(solution)/shard_map/all_to_all | solution.py:29
  193.1 5.4 %convolution_bitcast_fusion = f32[8,128,1024]{2,1,0:T(8,128)} fusion(bf16[8,128,1024,1]{2,1,0,3:T(8,128)(2,1)} %bitcast.31, bf16[8,16,8,8,128]{4,3,0,2,1:T(8,128)(2,1)S(1)} %bitcast.30), kind=kOutput, calls=%fused_computation | convolution fusion | flops 2147483648 | bytes 8388608 | tf_op jit(solution)/shard_map/ijab,jbk->iak/dot_general | solution.py:32
  198.5 0.0 reduce-scatter.2.cloned.1.call-update
  198.5 75.9 %reduce-scatter.2.cloned.1.call-done = f32[8,8,1024]{2,1,0:T(8,128)} async-done(((f32[8,128,1024]{2,1,0:T(8,128)}), f32[8,8,1024]{2,1,0:T(8,128)}) %reduce-scatter.2.cloned.1.call-update) | async-done | bytes 262160 | tf_op jit(solution)/shard_map/reduce_scatter | solution.py:33
  (1 shorter events, 0.0 us)
Async XLA Ops:
  6.5 55.6 %all-gather.6.cloned.1.call-start = ((), (), s32[]{:S(2)}) async-start(), calls=%async_computation.3 | async-start | bytes 9437184 | tf_op jit(solution)/shard_map/all_gather | solution.py:23
  7.4 2.5 copy-start.1
  7.4 2.9 %copy-start = (bf16[1024,256]{1,0:T(8,128)(2,1)S(1)}, bf16[1024,256]{1,0:T(8,128)(2,1)}, u32[]{:S(2)}) copy-start(bf16[1024,256]{1,0:T(8,128)(2,1)} %param.5) | copy-start | bytes 1572868
  9.9 133.2 %all-gather.4.cloned.1.call-start = ((), (), s32[]{:S(2)}) async-start(), calls=%async_computation.2 | async-start | bytes 8912896 | tf_op jit(solution)/shard_map/all_gather | solution.py:20
  11.3 159.9 %all-gather.8.cloned.1.call-start = ((), (), s32[]{:S(2)}) async-start(), calls=%async_computation.4 | async-start | bytes 2359296 | tf_op jit(solution)/shard_map/all_gather | solution.py:30
  159.3 33.8 %all-to-all-start = ((bf16[8,128,8,128]{3,2,0,1:T(8,128)(2,1)}), bf16[8,128,8,128]{3,2,0,1:T(8,128)(2,1)S(1)}, u32[]{:S(2)}, u32[]{:S(2)}) async-start(bf16[8,128,8,128]{3,2,0,1:T(8,128)(2,1)} %copy.9), calls=%async_computation | async-start | bytes 4194304 | tf_op jit(solution)/shard_map/all_to_all | solution.py:29
  164.2 110.3 %reduce-scatter.2.cloned.1.call-start = ((), (), s32[]{:S(2)}) async-start(), calls=%async_computation.5 | async-start | bytes 4456448 | tf_op jit(solution)/shard_map/reduce_scatter | solution.py:33
Sparse Core Ops, SparseCore 0:
  10.0 52.1 all-gather.5
  64.3 78.7 all-gather.3
  144.7 26.4 all-gather.7
  198.7 75.7 reduce-scatter.1
where the time goes:
time: 281 us
  waiting for transfers between devices  236 us (84%)
  matrix products  19.1 us (7%)
  between operations  13.2 us (5%)
  starting transfers between devices  5.07 us (2%)
  other arithmetic  3.97 us (1%)
  local copies, waits for them, and re-layouts  3.2 us (1%)
    all_gather x1, waiting for transfers between devices, body(): gathered = lax.all_gather(masked_left, 'col', axis=1, tiled=True)  80.9 us
    reduce_scatter x1, waiting for transfers between devices, body(): return lax.psum_scatter(cycle_terms, 'col', scatter_dimension=1, tiled=True)  75.9 us
    all_gather x1, waiting for transfers between devices, body(): lax.all_gather(masked_right, 'row', axis=0, tiled=True)  50.1 us
    all_to_all x1, waiting for transfers between devices, body(): lax.all_to_all(pair_block, 'col', split_axis=1, concat_axis=2, tiled=True)  21.9 us
    dot_general x1, matrix products, body(): jnp.dot(gathered, lax.all_gather(masked_right, 'row', axis=0, tiled=True)...  13.7 us
    all_gather x1, waiting for transfers between devices, body(): piece = lax.all_gather(cycle_weight, 'row', axis=1, tiled=True)  6.95 us
  transfers between devices with their start and end apart: 5, of which 5 were waited for; matrix products, arithmetic and copies ran while one was open for 6% of the time, Pallas kernels for 0%

commit v1 on v0

--- a/solution.py
+++ b/solution.py
@@ -5,6 +5,11 @@
 
 JOCC = 128
 VIRT_B = 128
+
+
+def swapped_in(x, axis, dim):
+    sent = jnp.stack([x] * lax.axis_size(axis))
+    return jnp.concatenate(lax.all_to_all(sent, axis, 0, 0), axis=dim)
 
 
 def apply_mask(tiles, mask):
@@ -27,7 +32,7 @@
     vir_local = right_mask.shape[1]
     pair_block = totals.astype(jnp.bfloat16).reshape(occ_local, JOCC, vir_local, VIRT_B)
     relaid = lax.all_to_all(pair_block, "col", split_axis=1, concat_axis=2, tiled=True)
-    piece = lax.all_gather(cycle_weight, "row", axis=1, tiled=True)
+    piece = swapped_in(cycle_weight, "row", 1)
     operand = piece.reshape(piece.shape[0] // VIRT_B, VIRT_B, piece.shape[1])
     cycle_terms = jnp.einsum("ijab,jbk->iak", relaid, operand, preferred_element_type=jnp.float32)
     return lax.psum_scatter(cycle_terms, "col", scatter_dimension=1, tiled=True)

time: 281 us -> 300 us (1.068)
  local copies, waits for them, and re-layouts: 3.2 us -> 10.3 us
  waiting for transfers between devices: 236 us -> 243 us
  starting transfers between devices: 5.07 us -> 9.46 us
    all_gather x1, waiting for transfers between devices: 50.1 us -> 62.5 us  [body(): lax.all_gather(masked_right, 'row', axis=0, tiled=True)]
    all_gather x1 -> x0, waiting for transfers between devices: 6.95 us -> none  [body(): piece = lax.all_gather(cycle_weight, 'row', axis=1, tiled=True)]
    another operation x0 -> x2, local copies, waits for them, and re-layouts: none -> 4.41 us  [the longest x1 2.82 us: body(): operand = piece.reshape(piece.shape[0] // VIRT_B, VIRT_B, piece.shape[1])]
    all_to_all x0 -> x1, starting transfers between devices: none -> 4.38 us  [swapped_in(): return jnp.concatenate(lax.all_to_all(sent, axis, 0, 0), axis=dim)]
  transfers between devices with their start and end apart: 5 -> 5, of which waited for: 5 -> 4; matrix products, arithmetic and copies ran while one was open for 6% -> 8% of each run, Pallas kernels for 0% -> 0%
where the time goes in v1:
time: 300 us; the launch traced here: 299 us
  waiting for transfers between devices  243 us (81%)
  matrix products  19.1 us (6%)
  between operations  13.2 us (4%)
  local copies, waits for them, and re-layouts  10.3 us (3%)
  starting transfers between devices  9.46 us (3%)
  other arithmetic  3.97 us (1%)
    all_gather x1, waiting for transfers between devices, body(): gathered = lax.all_gather(masked_left, 'col', axis=1, tiled=True)  81.3 us
    reduce_scatter x1, waiting for transfers between devices, body(): return lax.psum_scatter(cycle_terms, 'col', scatter_dimension=1, tiled=True)  76 us
    all_gather x1, waiting for transfers between devices, body(): lax.all_gather(masked_right, 'row', axis=0, tiled=True)  62.5 us
    all_to_all x1, waiting for transfers between devices, body(): lax.all_to_all(pair_block, 'col', split_axis=1, concat_axis=2, tiled=True)  23.4 us
    dot_general x1, matrix products, body(): jnp.dot(gathered, lax.all_gather(masked_right, 'row', axis=0, tiled=True)...  13.7 us
  transfers between devices with their start and end apart: 5, of which 4 were waited for; matrix products, arithmetic and copies ran while one was open for 8% of the time, Pallas kernels for 0%

profile of v1, /device:TPU:0, one launch (start us, length us, event | category | flops | bytes accessed | tf_op | source)
XLA Modules:
  0.0 299.3 jit_solution(7338317515574909082)
XLA Ops:
  6.5 0.0 all-gather.5.cloned.1.call-start
  6.5 0.7 convert_element_type.12
  7.2 0.2 mul.25
  7.4 0.0 copy-start.2
  7.4 0.0 copy-start
  7.5 2.4 bitcast_multiply_fusion
  9.9 0.0 copy-start.1
  9.9 0.0 all-gather.5.cloned.1.call-update
  9.9 0.0 all-gather.3.cloned.1.call-start
  9.9 0.0 copy-done.2
  9.9 0.1 copy.8
  10.0 0.3 mul.22
  10.4 0.0 copy-done
  10.4 0.9 bitcast_multiply_fusion.1
  11.3 0.0 all-gather.3.cloned.1.call-update
  11.3 0.0 copy-done.1
  11.3 1.6 stack.2
  12.9 4.4 %all-to-all-start.1 = ((bf16[8,1024,128]{2,1,0:T(8,128)(2,1)}), bf16[8,1024,128]{2,1,0:T(8,128)(2,1)S(1)}, u32[]{:S(2)}, u32[]{:S(2)}) async-start(bf16[8,1024,128]{2,1,0:T(8,128)(2,1)} %stack.2), calls=%async_computation.1 | async-start | bytes 4194304 | tf_op jit(solution)/shard_map/all_to_all | solution.py:12
  17.3 62.5 %all-gather.5.cloned.1.call-done = bf16[4096,1024]{1,0:T(8,128)(2,1)} async-done(((bf16[512,1024]{1,0:T(8,128)(2,1)}), bf16[4096,1024]{1,0:T(8,128)(2,1)}) %all-gather.5.cloned.1.call-update) | async-done | bytes 8388624 | tf_op jit(solution)/shard_map/all_gather | solution.py:28
  79.8 81.3 %all-gather.3.cloned.1.call-done = bf16[1024,4096]{1,0:T(8,128)(2,1)} async-done(((bf16[1024,256]{1,0:T(8,128)(2,1)}), bf16[1024,4096]{1,0:T(8,128)(2,1)}) %all-gather.3.cloned.1.call-update) | async-done | bytes 8388624 | tf_op jit(solution)/shard_map/all_gather | solution.py:25
  161.1 13.7 %convert_bitcast_fusion = bf16[128,8,8,128]{3,1,2,0:T(8,128)(2,1)S(1)} fusion(bf16[1024,4096]{1,0:T(8,128)(2,1)} %all-gather.3.cloned.1.call-done, bf16[4096,1024]{1,0:T(8,128)(2,1)} %all-gather.5.cloned.1.call-done), kind=kOutput, calls=%fused_computation.3 | convolution fusion | flops 8590983168 | bytes 18874368 | tf_op jit(solution)/shard_map/dot_general | solution.py:26
  174.7 0.6 copy.15
  175.4 1.9 copy.9
  177.3 0.0 all-to-all-done.1
  177.3 5.0 %all-to-all-start = ((bf16[8,128,8,128]{3,2,0,1:T(8,128)(2,1)}), bf16[8,128,8,128]{3,2,0,1:T(8,128)(2,1)}, u32[]{:S(2)}, u32[]{:S(2)}) async-start(bf16[8,128,8,128]{3,2,0,1:T(8,128)(2,1)} %copy.9), calls=%async_computation | async-start | bytes 4194304 | tf_op jit(solution)/shard_map/all_to_all | solution.py:34
  182.3 0.0 reduce-scatter.2.cloned.1.call-start
  182.4 2.7 copy.11
  185.0 2.8 reshape.20
  187.8 23.4 %all-to-all-done = bf16[8,128,8,128]{3,2,0,1:T(8,128)(2,1)} async-done(((bf16[8,128,8,128]{3,2,0,1:T(8,128)(2,1)}), bf16[8,128,8,128]{3,2,0,1:T(8,128)(2,1)}, u32[]{:S(2)}, u32[]{:S(2)}) %all-to-all-start) | async-done | bytes 2097184 | tf_op jit(solution)/shard_map/all_to_all | solution.py:34
  211.2 5.5 %convolution_bitcast_fusion = f32[8,128,1024]{2,1,0:T(8,128)} fusion(bf16[8,128,1024,1]{2,1,0,3:T(8,128)(2,1)S(1)} %reshape.20, bf16[8,16,8,8,128]{4,3,0,2,1:T(8,128)(2,1)} %bitcast), kind=kOutput, calls=%fused_computation | convolution fusion | flops 2147483648 | bytes 8388608 | tf_op jit(solution)/shard_map/ijab,jbk->iak/dot_general | solution.py:37
  216.7 0.0 reduce-scatter.2.cloned.1.call-update
  216.7 76.0 %reduce-scatter.2.cloned.1.call-done = f32[8,8,1024]{2,1,0:T(8,128)} async-done(((f32[8,128,1024]{2,1,0:T(8,128)}), f32[8,8,1024]{2,1,0:T(8,128)}) %reduce-scatter.2.cloned.1.call-update) | async-done | bytes 262160 | tf_op jit(solution)/shard_map/reduce_scatter | solution.py:38
  (1 shorter events, 0.0 us)
Async XLA Ops:
  6.5 73.2 %all-gather.5.cloned.1.call-start = ((), (), s32[]{:S(2)}) async-start(), calls=%async_computation.4 | async-start | bytes 9437184 | tf_op jit(solution)/shard_map/all_gather | solution.py:28
  7.4 2.5 copy-start.2
  7.4 2.9 copy-start
  9.9 1.5 copy-start.1
  9.9 151.2 %all-gather.3.cloned.1.call-start = ((), (), s32[]{:S(2)}) async-start(), calls=%async_computation.3 | async-start | bytes 8912896 | tf_op jit(solution)/shard_map/all_gather | solution.py:25
  12.9 164.4 %all-to-all-start.1 = ((bf16[8,1024,128]{2,1,0:T(8,128)(2,1)}), bf16[8,1024,128]{2,1,0:T(8,128)(2,1)S(1)}, u32[]{:S(2)}, u32[]{:S(2)}) async-start(bf16[8,1024,128]{2,1,0:T(8,128)(2,1)} %stack.2), calls=%async_computation.1 | async-start | bytes 4194304 | tf_op jit(solution)/shard_map/all_to_all | solution.py:12
  177.3 33.9 %all-to-all-start = ((bf16[8,128,8,128]{3,2,0,1:T(8,128)(2,1)}), bf16[8,128,8,128]{3,2,0,1:T(8,128)(2,1)}, u32[]{:S(2)}, u32[]{:S(2)}) async-start(bf16[8,128,8,128]{3,2,0,1:T(8,128)(2,1)} %copy.9), calls=%async_computation | async-start | bytes 4194304 | tf_op jit(solution)/shard_map/all_to_all | solution.py:34
  182.3 110.5 %reduce-scatter.2.cloned.1.call-start = ((), (), s32[]{:S(2)}) async-start(), calls=%async_computation.5 | async-start | bytes 4456448 | tf_op jit(solution)/shard_map/reduce_scatter | solution.py:38
Sparse Core Ops, SparseCore 0:
  10.0 69.7 all-gather.4
  81.9 79.1 all-gather.2
  216.8 75.8 reduce-scatter.1
